TPU v7x, 32 devices: a whole 2x2x4 slice. The times are simulated.
32 devices in a mesh: grp: 8 (over z, x), agg: 4 (over y, core).
Axes of the slice: x: 2, y: 2, z: 4, core: 2. Of those that a mesh axis runs over, the one named last changes fastest.
Arguments:
- solution: float32 [128, 32, 128], P('grp', 'agg'), may hold values from -6 to 6
- source_term: float32 [128, 32, 128], P('grp', 'agg'), may hold values from -6 to 6
- face_x: float32 [128, 32, 128], P('grp', 'agg'), may hold values from 0.5 to 2
- face_y: float32 [128, 32, 128], P('grp', 'agg'), may hold values from 0.5 to 2
- face_z: float32 [128, 32, 128], P('grp', 'agg'), may hold values from 0.5 to 2
Outputs:
- correction: float32 [64, 16, 64], P('grp', 'agg')
All inputs are finite; a program needn't handle non-finite values.
Results may differ from a plain program's by a relative error of at most 0.0003.
Values sent between devices are 32-bit elements; how exact they have to be, the bound alone decides.
A program may use at most 64 MiB of HBM per device.

v0:
```python
import functools

import jax
import jax.numpy as jnp
import ml_dtypes
import numpy as np
from jax import lax
from jax.experimental import pallas as pl
from jax.experimental.pallas import tpu as pltpu
from jax.sharding import PartitionSpec as P

LANES = 128
SWEEPS = 2
MESH = pl.DeviceIdType.MESH


class Sizes:
    def __init__(self, groups, members, block):
        self.G, self.A = groups, members
        self.X, self.Y, self.Z = block
        self.merges = members.bit_length() - 1
        self.f = 2 ** (self.merges - 1)
        self.b = 2**self.merges
        self.xm, self.ym, self.zm = self.X // self.f, self.Y // self.f, self.Z // self.f
        self.xb, self.zb = self.X // self.b, self.Z // self.b
        self.yb = max(1, self.Y // self.b)
        self.YM, self.YB = self.A * self.ym, self.A * self.Y // self.b
        self.q = self.A * self.yb // self.YB
        self.h = -(-(SWEEPS + 1) // self.xb)
        self.S = 2 * self.h + 1
        self.NXB = self.G * self.xb
        self.XBP = -(-self.S * self.xb // 8) * 8
        self.XMP = -(-(self.xm + 2 * SWEEPS) // 8) * 8
        self.RM = -(-self.ym * self.xm // 8) * 8
        self.RB = -(-self.yb * self.xb // 8) * 8
        self.per = LANES // self.zb
        self.NL = self.A * self.yb * self.zb // LANES


def bf16_parts(table):
    first = table.astype(ml_dtypes.bfloat16)
    second = (table - first.astype(np.float64)).astype(ml_dtypes.bfloat16)
    return np.stack([first, second])


def real_basis(count):
    at = np.arange(count)[:, None]
    mode = np.arange(count)
    wave = (mode + 1) // 2
    angle = 2 * np.pi * ((at * wave[None, :]) % count) / count
    basis = np.where(mode[None, :] % 2 == 1, np.cos(angle), np.sin(angle)) * np.sqrt(2.0 / count)
    basis[:, 0] = np.sqrt(1.0 / count)
    if count % 2 == 0:
        basis[:, count - 1] = np.sqrt(1.0 / count) * (1 - 2 * (np.arange(count) % 2))
    return basis, wave


def tables(s):
    left = np.zeros((4, s.RM + s.RB, s.X * s.Y))
    for x in range(s.X):
        for y in range(s.Y):
            for base, f, xn, in ((0, s.f, s.xm), (s.RM, s.b, s.xb)):
                row, col = base + (y // f) * xn + x // f, x * s.Y + y
                last_x, last_y = x % f == f - 1, y % f == f - 1 or (f > s.Y and y == s.Y - 1)
                left[0, row, col] = 1 / f**2
                left[1, row, col] = last_x / f
                left[2, row, col] = last_y / f
                left[3, row, col] = 1 / f**2
    right = np.zeros((2, s.Z, 2 * LANES))
    for lane in range(LANES):
        for base, f, zn in ((0, s.f, s.zm), (LANES, s.b, s.zb)):
            z = lane % zn
            right[0, z * f : (z + 1) * f, base + lane] = 1 / f
            right[1, (z + 1) * f - 1, base + lane] = 1
    qx, wx = real_basis(s.NXB)
    qy, wy = real_basis(s.YB)
    qz, wz = real_basis(s.zb)
    rows = np.arange(s.A * s.yb) // s.q
    to_modes = np.einsum("yk,zl->yzkl", qy[rows], qz).reshape(s.NL * LANES, s.YB * s.zb)
    copies = np.arange(LANES) % s.zb
    from_modes = np.einsum("yk,zl->klyz", qy, qz[copies]).reshape(s.YB * s.zb, s.YB * LANES)
    spread = np.einsum("ay,zl->azyl", rows[:, None] == np.arange(s.YB), np.arange(s.zb)[:, None] == copies[None, :])
    spread = spread.reshape(s.NL * LANES, s.YB * LANES).astype(np.float64)

    def eigen(wave, count):
        return 2.0 - 2.0 * np.cos(2.0 * np.pi * wave / count)

    symbol = (
        eigen(wx, s.NXB)[:, None, None] + eigen(wy, s.YB)[None, :, None] + eigen(wz, s.zb)[None, None, :]
    ).reshape(s.NXB, -1) * 0.25**s.merges
    symbol[0, 0] = 1.0
    inverse = 1.0 / symbol
    inverse[0, 0] = 0.0
    near = (np.arange(s.G)[:, None] * s.xb - s.h * s.xb + np.arange(s.XBP)[None, :]) % s.NXB
    qx_near = qx[near]
    pick = (near[:, :, None] == np.arange(s.NXB)).astype(np.float32)
    from_x = np.concatenate([qx_near, pick], 2).astype(np.float32)
    grow_x = np.zeros((s.XMP, s.XBP))
    for row in range(s.XMP):
        grow_x[row, min(s.h * s.xb + (row - SWEEPS) // 2, s.XBP - 1)] = 1
    grow_x = np.kron(np.eye(s.YB), grow_x)
    grow_z = np.zeros((LANES, LANES))
    for lane in range(LANES):
        grow_z[(lane % s.zm) // 2, lane] = 1
    bf = lambda t: t.astype(ml_dtypes.bfloat16)
    return (
        bf(left), bf(right), bf16_parts(to_modes), bf16_parts(from_modes), bf(spread),
        qx.T.astype(np.float32), inverse.astype(np.float32), from_x, bf(grow_x), bf(grow_z),
    )


def cut(value, count):
    parts = []
    for _ in range(count):
        part = value.astype(jnp.bfloat16).astype(jnp.float32)
        parts.append(part)
        value = value - part
    return parts


def dot(one, two):
    return jnp.dot(one, two, preferred_element_type=jnp.float32)


def right_exact(value, table, count=3):
    rows = value.shape[0]
    product = dot(jnp.concatenate(cut(value, count), 0).astype(jnp.bfloat16), table)
    return sum(product[i * rows : (i + 1) * rows] for i in reversed(range(count)))


def left_exact(table, value, count=3):
    columns = value.shape[1]
    product = dot(table, jnp.concatenate(cut(value, count), 1).astype(jnp.bfloat16))
    return sum(product[:, i * columns : (i + 1) * columns] for i in reversed(range(count)))


def right_parts(value, high, low):
    rows = value.shape[0]
    stacked = jnp.concatenate(cut(value, 2), 0).astype(jnp.bfloat16)
    by_high = dot(stacked, high)
    by_low = dot(stacked, low)
    return by_low[:rows] + by_high[rows:] + by_low[rows:] + by_high[:rows]


def full_dot(one, two):
    return jnp.dot(one, two, precision=lax.Precision.HIGHEST, preferred_element_type=jnp.float32)


def turned(value, step, axis):
    if axis == 0:
        return jnp.concatenate([value[step:], value[:step]], 0)
    return pltpu.roll(value, (-step) % value.shape[axis], axis)


def sweeps(current, residual, faces, factor):
    along = (1, 0, 2)
    below = [turned(face, -1, d) for face, d in zip(faces, along)]
    diagonal = sum(face + under for face, under in zip(faces, below))
    scale = (2.0 / 3.0) / (factor * diagonal)
    for _ in range(SWEEPS):
        applied = diagonal * current
        for face, under, d in zip(faces, below, along):
            applied = applied - face * turned(current, 1, d) - under * turned(current, -1, d)
        current = current + scale * (residual - factor * applied)
    return current


def each(count, body):
    if count <= 64:
        for i in range(count):
            body(i)
    else:
        lax.fori_loop(0, count, lambda i, c: (body(i), c)[1], 0)


def kernel(
    s, operand_count, *refs
):
    operands, out, held = refs[:operand_count], refs[operand_count], refs[operand_count + 1 : 2 * operand_count + 1]
    body(s, operands, out, held, *refs[2 * operand_count + 1 :])


def body(
    s, operands, out, held,
    x_low, x_high, y_low, y_high, y_low_src, y_high_src,
    coef_own, coef_side, coef_side_src, coef_bot,
    res_own, res_side, res_side_src, gathered,
    bottom_all, mid_faces, mid_res, bot_faces, final,
    send, recv, loaded,
):
    sol, src, fx, fy, fz, left, right, to_modes, from_modes, spread, qx_t, inverse, from_x, grow_x, grow_z = held
    g, a = lax.axis_index("grp"), lax.axis_index("agg")
    me = g * s.A + a
    others = s.G * s.A - 1

    def shifted(i):
        at = lax.rem(me + 1 + i, s.G * s.A)
        return {"grp": at // s.A, "agg": lax.rem(at, s.A)}

    barrier = pltpu.get_barrier_semaphore()
    each(others, lambda i: pl.semaphore_signal(barrier, inc=1, device_id=shifted(i), device_id_type=MESH))

    order = (0, 3, 2, 4, 5, 6, 1, 7, 10, 11, 12, 8, 9, 13, 14)
    loads = [pltpu.make_async_copy(operands[i], held[i], loaded.at[i]) for i in range(len(held))]
    for i in order:
        loads[i].start()

    def ready(*which):
        for i in which:
            loads[i].wait()

    ready(0, 3)
    y_low_src[0] = sol[:, s.Y - 1, :]
    y_low_src[1] = fy[:, s.Y - 1, :]
    y_high_src[...] = sol[:, 0, :]

    def put(src_ref, dst_ref, kind, to):
        copy = pltpu.make_async_remote_copy(
            src_ref=src_ref, dst_ref=dst_ref, send_sem=send.at[kind], recv_sem=recv.at[kind],
            device_id=to, device_id_type=MESH,
        )
        copy.start()

    up, down = lax.rem(g + 1, s.G), lax.rem(g + s.G - 1, s.G)
    right_of, left_of = lax.rem(a + 1, s.A), lax.rem(a + s.A - 1, s.A)

    ready(2)
    pl.semaphore_wait(barrier, others)
    put(sol.at[s.X - 1], x_low.at[0], 0, {"grp": up, "agg": a})
    put(fx.at[s.X - 1], x_low.at[1], 1, {"grp": up, "agg": a})
    put(sol.at[0], x_high, 2, {"grp": down, "agg": a})
    put(y_low_src, y_low, 3, {"grp": g, "agg": right_of})
    put(y_high_src, y_high, 4, {"grp": g, "agg": left_of})

    ready(4, 5, 6)
    flat = lambda ref: ref[...].reshape(s.X * s.Y, s.Z)
    half = s.RM + s.RB
    rows = [left_exact(left[d + 1], flat(ref)) for d, ref in enumerate((fx, fy, fz))]
    both = right_exact(jnp.concatenate(rows[:2], 0), right[0])
    coarse = [both[:half], both[half:], right_exact(rows[2], right[1])]
    for d in range(3):
        mid, bottom = coarse[d][: s.RM, :LANES], coarse[d][s.RM :, LANES:]
        if d == 1 and s.q > 1:
            bottom = jnp.where(lax.rem(a, s.q) == s.q - 1, bottom, 0.0)
        for y in range(s.ym):
            plane = mid[y * s.xm : (y + 1) * s.xm]
            coef_own[a * s.ym + y, d] = plane
            coef_side_src[0, y, d] = plane[s.xm - SWEEPS :]
            coef_side_src[1, y, d] = plane[:SWEEPS]
        for y in range(s.yb):
            coef_bot[(s.h * s.A + a) * s.yb + y, d] = bottom[y * s.xb : (y + 1) * s.xb]

    own_rows = pl.ds(a * s.ym, s.ym)
    bot_rows = lambda k: pl.ds((k * s.A + a) * s.yb, s.yb)

    def to_members(body):
        each(s.A - 1, lambda i: body({"grp": g, "agg": lax.rem(a + 1 + i, s.A)}))

    def to_sides(body):
        for side, to in ((0, up), (1, down)):
            each(s.A, lambda i: body(side, {"grp": to, "agg": lax.rem(a + i, s.A)}))

    to_sides(lambda side, to: put(coef_side_src.at[side], coef_side.at[side, own_rows], 5, to))
    to_members(lambda to: put(coef_own.at[own_rows], coef_own.at[own_rows], 6, to))
    bot_src = coef_bot.at[bot_rows(s.h)]
    for d in range(-s.h, s.h + 1):
        to_g = lax.rem(g + d + s.G, s.G)
        send_bot = lambda to: put(bot_src, coef_bot.at[bot_rows(s.h - d)], 7, to)
        if d == 0:
            to_members(send_bot)
        else:
            each(s.A, lambda i: send_bot({"grp": to_g, "agg": lax.rem(a + i, s.A)}))

    def got(ref, kind, sems=recv):
        pltpu.make_async_copy(ref, ref, sems.at[kind]).wait()

    here = sol[...]
    f_x, f_y, f_z = fx[...], fy[...], fz[...]
    z_part = f_z * (here - pltpu.roll(here, s.Z - 1, 2))
    z_part = z_part - pltpu.roll(z_part, 1, 2)
    got(x_low.at[0], 0)
    got(x_low.at[1], 1)
    got(x_high, 2)
    flux = f_x * (here - jnp.concatenate([here[1:], x_high[...][None]], 0))
    edge = x_low[1] * (x_low[0] - here[0])
    x_part = flux - jnp.concatenate([edge[None], flux[:-1]], 0)
    got(y_low, 3)
    got(y_high, 4)
    row = lax.broadcasted_iota(jnp.int32, here.shape, 1)
    above = jnp.where(row == s.Y - 1, y_high[...][:, None, :], pltpu.roll(here, s.Y - 1, 1))
    flux = f_y * (here - above)
    edge = (y_low[1] * (y_low[0] - here[:, 0, :]))[:, None, :]
    y_part = flux - jnp.where(row == 0, edge, pltpu.roll(flux, 1, 1))
    ready(1)
    residual = src[...] - (x_part + y_part + z_part)

    coarse_res = right_exact(left_exact(left[0], residual.reshape(s.X * s.Y, s.Z)), right[0])
    mid, bottom = coarse_res[: s.RM, :LANES], coarse_res[s.RM :, LANES:]
    group = lax.broadcasted_iota(jnp.int32, (s.xb, LANES), 1) // s.zb
    slot = jnp.zeros((s.xb, LANES), jnp.float32)
    for y in range(s.yb):
        slot = slot + jnp.where(
            group == lax.rem(a * s.yb + y, s.per), bottom[y * s.xb : (y + 1) * s.xb], 0.0
        )
    gathered[me] = slot
    each(others, lambda i: put(gathered.at[me], gathered.at[me], 10, shifted(i)))
    for y in range(s.ym):
        plane = mid[y * s.xm : (y + 1) * s.xm]
        res_own[a * s.ym + y] = plane
        res_side_src[0, y] = plane[s.xm - SWEEPS :]
        res_side_src[1, y] = plane[:SWEEPS]
    to_sides(lambda side, to: put(res_side_src.at[side], res_side.at[side, own_rows], 8, to))
    to_members(lambda to: put(res_own.at[own_rows], res_own.at[own_rows], 9, to))

    got(coef_side, 5)
    part = coef_own.at[pl.ds(0, (s.A - 1) * s.ym)]
    got(part, 6)
    got(coef_bot.at[pl.ds(0, (s.S * s.A - 1) * s.yb)], 7)
    mid_faces[...] = jnp.ones(mid_faces.shape, jnp.float32)
    bot_faces[...] = jnp.ones(bot_faces.shape, jnp.float32)
    for d in range(3):
        mid_faces[d, :, 0:SWEEPS, :] = coef_side[0, :, d]
        mid_faces[d, :, SWEEPS : SWEEPS + s.xm, :] = coef_own[:, d]
        mid_faces[d, :, SWEEPS + s.xm : 2 * SWEEPS + s.xm, :] = coef_side[1, :, d]
        for k in range(s.S):
            for y in range(s.YB):
                total = coef_bot[k * s.A * s.yb + y * s.q, d]
                for i in range(1, s.q):
                    total = total + coef_bot[k * s.A * s.yb + y * s.q + i, d]
                bot_faces[d, y, k * s.xb : (k + 1) * s.xb, :] = total

    got(gathered.at[pl.ds(0, others)], 10)
    chunk = s.A // s.NL
    for i in range(s.G):
        for k in range(s.NL):
            total = gathered[i * s.A + k * chunk]
            for j in range(1, chunk):
                total = total + gathered[i * s.A + k * chunk + j]
            bottom_all[i * s.xb : (i + 1) * s.xb, k * LANES : (k + 1) * LANES] = total
    everything = bottom_all[...]
    ready(7, 8, 9, 10, 11, 12, 13, 14)
    modes = right_parts(everything, to_modes[0], to_modes[1])
    modes = full_dot(qx_t[...], modes) * inverse[...]
    near = from_x[g]
    field = right_parts(full_dot(near[:, : s.NXB], modes), from_modes[0], from_modes[1])
    source = right_exact(full_dot(near[:, s.NXB :], everything), spread[...])
    planes = lambda wide: jnp.stack([wide[:, y * LANES : (y + 1) * LANES] for y in range(s.YB)])
    field = sweeps(planes(field), planes(source), [bot_faces[d] for d in range(3)], 0.25**s.merges)

    field = right_exact(field.reshape(s.YB * s.XBP, LANES), grow_z[...])
    field = left_exact(grow_x[...], field).reshape(s.YB, s.XMP, LANES)
    field = jnp.stack([field[y // 2] for y in range(s.YM)])
    got(res_side, 8)
    got(res_own.at[pl.ds(0, (s.A - 1) * s.ym)], 9)
    mid_res[...] = jnp.zeros(mid_res.shape, jnp.float32)
    mid_res[:, 0:SWEEPS, :] = res_side[0]
    mid_res[:, SWEEPS : SWEEPS + s.xm, :] = res_own[...]
    mid_res[:, SWEEPS + s.xm : 2 * SWEEPS + s.xm, :] = res_side[1]
    final[...] = sweeps(field, mid_res[...], [mid_faces[d] for d in range(3)], 0.25 ** (s.merges - 1))
    out[...] = final[own_rows, SWEEPS : SWEEPS + s.xm, : s.zm]

    sent = (
        x_high, x_high, x_high, y_low, y_high, coef_side, part, coef_bot.at[pl.ds(0, (s.S * s.A - 1) * s.yb)],
        res_side, res_own.at[pl.ds(0, (s.A - 1) * s.ym)], gathered.at[pl.ds(0, others)],
    )
    for kind, ref in enumerate(sent):
        got(ref, kind, send)


def local(s, constants, sol, src, fx, fy, fz):
    f32 = lambda *shape: pltpu.VMEM(shape, jnp.float32)
    total = s.G * s.A
    arrays = (sol, src, fx, fy, fz, *constants)
    result = pl.pallas_call(
        functools.partial(kernel, s, len(arrays)),
        out_shape=jax.ShapeDtypeStruct((s.ym, s.xm, s.zm), jnp.float32),
        in_specs=[pl.BlockSpec(memory_space=pltpu.HBM)] * len(arrays),
        out_specs=pl.BlockSpec(memory_space=pltpu.VMEM),
        scratch_shapes=[
            *[pltpu.VMEM(array.shape, array.dtype) for array in arrays],
            f32(2, s.Y, s.Z), f32(s.Y, s.Z), f32(2, s.X, s.Z), f32(s.X, s.Z), f32(2, s.X, s.Z), f32(s.X, s.Z),
            f32(s.YM, 3, s.xm, LANES), f32(2, s.YM, 3, SWEEPS, LANES), f32(2, s.ym, 3, SWEEPS, LANES),
            f32(s.S * s.A * s.yb, 3, s.xb, LANES),
            f32(s.YM, s.xm, LANES), f32(2, s.YM, SWEEPS, LANES), f32(2, s.ym, SWEEPS, LANES),
            f32(total, s.xb, LANES),
            f32(s.NXB, s.NL * LANES), f32(3, s.YM, s.XMP, LANES), f32(s.YM, s.XMP, LANES),
            f32(3, s.YB, s.XBP, LANES), f32(s.YM, s.XMP, LANES),
            pltpu.SemaphoreType.DMA((11,)),
            pltpu.SemaphoreType.DMA((11,)),
            pltpu.SemaphoreType.DMA((len(arrays),)),
        ],
        compiler_params=pltpu.CompilerParams(
            collective_id=0, has_side_effects=True
        ),
    )(*arrays)
    return jnp.transpose(result, (1, 0, 2))


def solution(mesh):
    groups, members = mesh.shape["grp"], mesh.shape["agg"]

    def whole(*arrays):
        nx, ny, nz = arrays[0].shape
        s = Sizes(groups, members, (nx // groups, ny // members, nz))
        constants = [jnp.asarray(t) for t in tables(s)]
        return jax.shard_map(
            functools.partial(local, s, constants),
            mesh=mesh,
            in_specs=(P("grp", "agg", None),) * 5,
            out_specs=P("grp", "agg", None),
            check_vma=False,
        )(*arrays)

    return whole
```

profile of v0, /device:TPU:0, one launch (start us, length us, event | category | flops | bytes accessed | tf_op | source)
XLA Modules:
  0.0 19.3 jit_solution(16038473754417725977)
XLA Ops:
  0.0 18.0 %shard_map.145 = f32[4,8,64]{2,1,0:T(8,128)} custom-call(f32[16,8,128]{2,1,0:T(8,128)} %refs_0_.1, f32[16,8,128]{2,1,0:T(8,128)} %refs_1_.1, f32[16,8,128]{2,1,0:T(8,128)} %refs_2_.1, f32[16,8,128]{2,1,0:T(8,128)} %refs_3_.1, f32[16,8,128]{2,1,0:T(8,128)} %refs_4_.1, bf16[4,40,128]{2,1,0:T(8,128)(2,1)} %constant.20.clone.refs_5_, ...), custom_call_target="tpu_custom_call" | custom-call | tf_op jit(solution)/shard_map/pallas_call | solution.py:374
  18.0 1.3 %copy.16 = f32[8,4,64]{2,1,0:T(4,128)} copy(f32[8,4,64]{2,0,1:T(8,128)} %bitcast.1) | data formatting | bytes 16384 | tf_op jit(solution)/shard_map/transpose | solution.py:396
where the time goes:
time: 19.5 us; the launch traced here: 19.3 us
  Pallas kernels  18 us (92%)
  local copies, waits for them, and re-layouts  1.33 us (7%)
    pallas_call x1, Pallas kernels, local(): pl.pallas_call(functools.partial(kernel, s, len(arrays)), out_shape=jax.S...  18 us
    transpose x1, local copies, waits for them, and re-layouts, local(): return jnp.transpose(result, (1, 0, 2))  1.33 us

commit v1 on v0

--- a/solution.py
+++ b/solution.py
@@ -197,13 +197,12 @@
         at = lax.rem(me + 1 + i, s.G * s.A)
         return {"grp": at // s.A, "agg": lax.rem(at, s.A)}
 
-    barrier = pltpu.get_barrier_semaphore()
-    each(others, lambda i: pl.semaphore_signal(barrier, inc=1, device_id=shifted(i), device_id_type=MESH))
-
     order = (0, 3, 2, 4, 5, 6, 1, 7, 10, 11, 12, 8, 9, 13, 14)
     loads = [pltpu.make_async_copy(operands[i], held[i], loaded.at[i]) for i in range(len(held))]
     for i in order:
         loads[i].start()
+    barrier = pltpu.get_barrier_semaphore()
+    each(others, lambda i: pl.semaphore_signal(barrier, inc=1, device_id=shifted(i), device_id_type=MESH))
 
     def ready(*which):
         for i in which:
@@ -214,25 +213,7 @@
     y_low_src[1] = fy[:, s.Y - 1, :]
     y_high_src[...] = sol[:, 0, :]
 
-    def put(src_ref, dst_ref, kind, to):
-        copy = pltpu.make_async_remote_copy(
-            src_ref=src_ref, dst_ref=dst_ref, send_sem=send.at[kind], recv_sem=recv.at[kind],
-            device_id=to, device_id_type=MESH,
-        )
-        copy.start()
-
-    up, down = lax.rem(g + 1, s.G), lax.rem(g + s.G - 1, s.G)
-    right_of, left_of = lax.rem(a + 1, s.A), lax.rem(a + s.A - 1, s.A)
-
-    ready(2)
-    pl.semaphore_wait(barrier, others)
-    put(sol.at[s.X - 1], x_low.at[0], 0, {"grp": up, "agg": a})
-    put(fx.at[s.X - 1], x_low.at[1], 1, {"grp": up, "agg": a})
-    put(sol.at[0], x_high, 2, {"grp": down, "agg": a})
-    put(y_low_src, y_low, 3, {"grp": g, "agg": right_of})
-    put(y_high_src, y_high, 4, {"grp": g, "agg": left_of})
-
-    ready(4, 5, 6)
+    ready(2, 4, 5, 6)
     flat = lambda ref: ref[...].reshape(s.X * s.Y, s.Z)
     half = s.RM + s.RB
     rows = [left_exact(left[d + 1], flat(ref)) for d, ref in enumerate((fx, fy, fz))]
@@ -249,6 +230,23 @@
             coef_side_src[1, y, d] = plane[:SWEEPS]
         for y in range(s.yb):
             coef_bot[(s.h * s.A + a) * s.yb + y, d] = bottom[y * s.xb : (y + 1) * s.xb]
+
+    def put(src_ref, dst_ref, kind, to):
+        copy = pltpu.make_async_remote_copy(
+            src_ref=src_ref, dst_ref=dst_ref, send_sem=send.at[kind], recv_sem=recv.at[kind],
+            device_id=to, device_id_type=MESH,
+        )
+        copy.start()
+
+    up, down = lax.rem(g + 1, s.G), lax.rem(g + s.G - 1, s.G)
+    right_of, left_of = lax.rem(a + 1, s.A), lax.rem(a + s.A - 1, s.A)
+
+    pl.semaphore_wait(barrier, others)
+    put(sol.at[s.X - 1], x_low.at[0], 0, {"grp": up, "agg": a})
+    put(fx.at[s.X - 1], x_low.at[1], 1, {"grp": up, "agg": a})
+    put(sol.at[0], x_high, 2, {"grp": down, "agg": a})
+    put(y_low_src, y_low, 3, {"grp": g, "agg": right_of})
+    put(y_high_src, y_high, 4, {"grp": g, "agg": left_of})
 
     own_rows = pl.ds(a * s.ym, s.ym)
     bot_rows = lambda k: pl.ds((k * s.A + a) * s.yb, s.yb)
@@ -357,7 +355,8 @@
     mid_res[:, SWEEPS : SWEEPS + s.xm, :] = res_own[...]
     mid_res[:, SWEEPS + s.xm : 2 * SWEEPS + s.xm, :] = res_side[1]
     final[...] = sweeps(field, mid_res[...], [mid_faces[d] for d in range(3)], 0.25 ** (s.merges - 1))
-    out[...] = final[own_rows, SWEEPS : SWEEPS + s.xm, : s.zm]
+    for y in range(s.ym):
+        out[:, y, :] = final[a * s.ym + y, SWEEPS : SWEEPS + s.xm, : s.zm]
 
     sent = (
         x_high, x_high, x_high, y_low, y_high, coef_side, part, coef_bot.at[pl.ds(0, (s.S * s.A - 1) * s.yb)],
@@ -373,7 +372,7 @@
     arrays = (sol, src, fx, fy, fz, *constants)
     result = pl.pallas_call(
         functools.partial(kernel, s, len(arrays)),
-        out_shape=jax.ShapeDtypeStruct((s.ym, s.xm, s.zm), jnp.float32),
+        out_shape=jax.ShapeDtypeStruct((s.xm, s.ym, s.zm), jnp.float32),
         in_specs=[pl.BlockSpec(memory_space=pltpu.HBM)] * len(arrays),
         out_specs=pl.BlockSpec(memory_space=pltpu.VMEM),
         scratch_shapes=[
@@ -393,7 +392,7 @@
             collective_id=0, has_side_effects=True
         ),
     )(*arrays)
-    return jnp.transpose(result, (1, 0, 2))
+    return result
 
 
 def solution(mesh):

time: 19.5 us -> 19.5 us (level)
    transpose x1 -> x0, local copies, waits for them, and re-layouts: 1.33 us -> none  [local(): return jnp.transpose(result, (1, 0, 2))]
    unnamed x0 -> x1, local copies, waits for them, and re-layouts: none -> 1.32 us
where the time goes in v1:
time: 19.5 us; the launch traced here: 19.3 us
  Pallas kernels  17.9 us (92%)
  local copies, waits for them, and re-layouts  1.32 us (7%)
    pallas_call x1, Pallas kernels, local(): pl.pallas_call(functools.partial(kernel, s, len(arrays)), out_shape=jax.S...  17.9 us
    unnamed x1, local copies, waits for them, and re-layouts  1.32 us

profile of v1, /device:TPU:0, one launch (start us, length us, event | category | flops | bytes accessed | tf_op | source)
XLA Modules:
  0.0 19.3 jit_solution(12638912277466631866)
XLA Ops:
  0.0 17.9 %shard_map.145 = f32[8,4,64]{2,1,0:T(4,128)} custom-call(f32[16,8,128]{2,1,0:T(8,128)} %refs_0_.1, f32[16,8,128]{2,1,0:T(8,128)} %refs_1_.1, f32[16,8,128]{2,1,0:T(8,128)} %refs_2_.1, f32[16,8,128]{2,1,0:T(8,128)} %refs_3_.1, f32[16,8,128]{2,1,0:T(8,128)} %refs_4_.1, bf16[4,40,128]{2,1,0:T(8,128)(2,1)} %constant.20.clone.refs_5_, ...), custom_call_target="tpu_custom_call" | custom-call | tf_op jit(solution)/shard_map/pallas_call | solution.py:373
  17.9 1.3 %copy.17 = f32[8,4,64]{2,1,0:T(4,128)} copy(f32[8,4,64]{2,1,0:T(4,128)} %shard_map.145) | data formatting | bytes 16384
